TPU v7x, 1024 devices: a whole 4x8x16 slice. The times are simulated.
1024 devices in a mesh: comp: 2 (over z_hi), tile: 512 (over x, z_lo, y, core).
Axes of the slice: x: 4, y: 8, z: 16 (z_hi: 2, z_lo: 8; z = z_hi * 8 + z_lo), core: 2. Of those that a mesh axis runs over, the one named last changes fastest.
Arguments:
- ocean_fields: float32 [2, 6, 64, 65536], P('comp', None, None, 'tile'), may hold values from -6 to 6, as said below
- tracers: float32 [19, 64, 65536], P(None, None, 'tile'), may hold values from -6 to 6
- reaction: float32 [19, 19], replicated, may hold values from -1.25 to 1.25
- wet_levels: int32 [65536], P('tile'), may hold values from 0 to 64, as said below
- neighbours: int32 [3, 65536], P(None, 'tile'), may hold values from 0 to 383, as said below
Outputs:
- ocean_out: float32 [2, 6, 64, 65536], P('comp', None, None, 'tile')
- chl_out: float32 [2, 64, 65536], P('comp', None, 'tile')
Inputs may be any that keep to these rules, and one draw needn't show every extreme that they name: `ocean_fields`: along the second dimension: temperature, salinity, eastward and northward velocity, a mixing index, and the shortwave flux, which lies between 0.2 and 2. `wet_levels`: 0 marks land; the share of land differs from tile to tile. `neighbours`: entry [k, c] gives the k-th neighbour of column c as a position in its tile's columns extended by 128 columns of each adjacent tile on both sides, the tiles closing into a loop: position p is the tile's column p - 128; no column is its own neighbour.
All inputs are finite; a program needn't handle non-finite values.
Results may differ from a plain program's by a relative error of at most 0.000061.
Values sent between devices are 32-bit elements; how exact they have to be, the bound alone decides.
A program may use at most 32 MiB of HBM per device.

v0:
```python
import math

import jax
import jax.numpy as jnp
from jax import lax
from jax.sharding import PartitionSpec as P

RIM = 128


ROTATE_COS = math.cos(0.3)
ROTATE_SIN = math.sin(0.3)


def padded(cells, sides, width):
    for axis, dim in sides:
        count = lax.axis_size(axis)
        head = lax.slice_in_dim(cells, 0, width, axis=dim)
        tail = lax.slice_in_dim(cells, cells.shape[dim] - width, cells.shape[dim], axis=dim)
        cells = jnp.concatenate(
            [
                lax.ppermute(tail, axis, [(i, (i + 1) % count) for i in range(count)]),
                cells,
                lax.ppermute(head, axis, [((i + 1) % count, i) for i in range(count)]),
            ],
            axis=dim,
        )
    return cells


def from_behind(block, axis, distance):
    devices = range(lax.axis_size(axis))
    route = [(i - distance, i) for i in devices if i - distance in devices]
    return lax.ppermute(block, axis, route)


def edge_weight(eastward, northward, face_index):
    angle = 2.0 * math.pi * face_index / 3.0
    return 0.05 + 0.25 * jax.nn.sigmoid(eastward * math.cos(angle) + northward * math.sin(angle))


def vertical_mix(state, mixing, active):
    diffusivity = 0.02 + 0.13 * jax.nn.sigmoid(mixing)
    link_weight = diffusivity[:-1] * active[:-1] * active[1:]
    link_flux = link_weight * (state[..., 1:, :] - state[..., :-1, :])
    zero_row = jnp.zeros_like(state[..., :1, :])
    upper_term = jnp.concatenate([link_flux, zero_row], axis=-2)
    lower_term = jnp.concatenate([zero_row, link_flux], axis=-2)
    return state + upper_term - lower_term


def transport(carried, extended, active, neighbours, weights):
    count = carried.shape[0]
    change = jnp.zeros_like(carried)
    for face_index in range(3):
        remote = jnp.take(extended, neighbours[face_index], axis=2)
        change = change + weights[face_index] * remote[count] * (remote[:count] - carried)
    return carried + active * change


def ocean_local(fields, chlorophyll, extended, active, neighbours):
    weights = []
    for face_index in range(3):
        face_weight = edge_weight(fields[2], fields[3], face_index)
        steady = jnp.full_like(face_weight, 0.15)
        weights.append(jnp.stack([face_weight, face_weight, steady, steady]))
    moved_state = transport(fields[:4], extended, active, neighbours, weights)
    rotated_east = ROTATE_COS * moved_state[2] + ROTATE_SIN * moved_state[3]
    rotated_north = -ROTATE_SIN * moved_state[2] + ROTATE_COS * moved_state[3]
    stacked = jnp.stack([moved_state[0], moved_state[1], rotated_east, rotated_north])
    stirred_condition = vertical_mix(stacked, fields[4], active)
    uppermost_layer = fields[5, 0]
    absorbed = 0.01 + 0.3 * jax.nn.softplus(chlorophyll)
    optical_depth = jnp.cumsum(absorbed, axis=0)
    bottom_light_flux = jnp.exp(-optical_depth)
    ceiling_light_flux = jnp.exp(-(optical_depth - absorbed))
    seawater_warmth = stirred_condition[0] + 4.0 * uppermost_layer * (
        ceiling_light_flux - bottom_light_flux
    )
    stratified_mass_profile = seawater_warmth - jnp.concatenate(
        [seawater_warmth[1:], seawater_warmth[-1:]], axis=0
    )
    sunlight_input = uppermost_layer * ceiling_light_flux
    advance_outcome = jnp.stack(
        [
            seawater_warmth,
            stirred_condition[1],
            stirred_condition[2],
            stirred_condition[3],
            stratified_mass_profile,
            sunlight_input,
        ]
    )
    return advance_outcome * active


def bgc_local(tracer_state, lagged, extended, reaction, active, neighbours):
    weights = [edge_weight(lagged[2], lagged[3], face_index) for face_index in range(3)]
    moved_state = transport(tracer_state, extended, active, neighbours, weights)
    stirred_condition = vertical_mix(moved_state, lagged[4], active)
    growth_rate = 0.5 * lagged[5] * jax.nn.sigmoid(lagged[0] + 0.5 * lagged[1])
    flat_state = jnp.tanh(stirred_condition).reshape(stirred_condition.shape[0], -1)
    growth = jnp.dot(
        reaction, flat_state, precision=lax.Precision.HIGHEST, preferred_element_type=jnp.float32
    ).reshape(stirred_condition.shape)
    return (stirred_condition + growth_rate * growth) * active


def full_exchange(packed):
    return padded(packed, (("tile", 2),), RIM)


def packed_rows(is_ocean, ocean_state, tracer_state):
    tracer_rows = tracer_state.shape[0]
    padding = jnp.zeros((tracer_rows - 4,) + ocean_state.shape[1:], jnp.float32)
    ocean_rows = jnp.concatenate([ocean_state[:4], padding], axis=0)
    return jnp.where(is_ocean, ocean_rows, tracer_state)


def step_rims(is_ocean, ocean_state, tracer_state, active):
    tracer_rows = tracer_state.shape[0]
    packed = packed_rows(is_ocean, ocean_state, tracer_state)
    extended = full_exchange(jnp.concatenate([packed, active[None]], axis=0))
    ocean_ext = jnp.concatenate([extended[:4], extended[tracer_rows:]], axis=0)
    return (ocean_ext, extended)


def per_device(ocean_fields, tracers, reaction, wet_levels, neighbours):
    is_ocean = lax.axis_index("comp") == 0
    level_index = jnp.arange(tracers.shape[1], dtype=jnp.int32)
    active = (level_index[:, None] < wet_levels[None, :]).astype(jnp.float32)
    fields = ocean_fields[0]
    ocean_ext, tracer_ext = step_rims(is_ocean, fields, tracers, active)

    def ocean_first():
        return (ocean_local(fields, tracers[0], ocean_ext, active, neighbours), tracers)

    def bgc_first():
        return (fields, bgc_local(tracers, fields, tracer_ext, reaction, active, neighbours))

    ocean_one, tracer_one = lax.cond(is_ocean, ocean_first, bgc_first)
    lagged_two = from_behind(ocean_one, "comp", 1)
    chl_arrived = from_behind(tracer_one[0], "comp", -1)
    ocean_ext, tracer_ext = step_rims(is_ocean, ocean_one, tracer_one, active)

    def ocean_second():
        return (ocean_local(ocean_one, chl_arrived, ocean_ext, active, neighbours), tracer_one)

    def bgc_second():
        return (
            ocean_one,
            bgc_local(tracer_one, lagged_two, tracer_ext, reaction, active, neighbours),
        )

    ocean_two, tracer_two = lax.cond(is_ocean, ocean_second, bgc_second)
    ocean_out = jnp.where(is_ocean, ocean_two, lagged_two)[None]
    chl_out = jnp.where(is_ocean, chl_arrived, tracer_two[0])[None]
    return (ocean_out, chl_out)


def solution(mesh):
    return jax.shard_map(
        per_device,
        mesh=mesh,
        in_specs=(
            P("comp", None, None, "tile"),
            P(None, None, "tile"),
            P(),
            P("tile"),
            P(None, "tile"),
        ),
        out_specs=(P("comp", None, None, "tile"), P("comp", None, "tile")),
        check_vma=False,
    )
```

profile of v0, /device:TPU:6, one launch (start us, length us, event | category | flops | bytes accessed | tf_op | source)
XLA Modules:
  0.0 110.2 jit_solution(2289960943675428738)
XLA Ops:
  0.6 0.0 copy-start.6
  0.6 1.1 copy.105
  1.7 0.9 copy.104
  2.7 0.0 copy-done.6
  2.7 0.1 pad_select_fusion.1
  2.8 0.1 pad_maximum_fusion.5
  2.8 1.9 %collective-permute-start = (f32[20,64,128]{2,1,0:T(8,128)S(1)}, f32[20,64,128]{2,1,0:T(8,128)S(1)}, u32[]{:S(2)}, u32[]{:S(2)}) collective-permute-start(f32[20,64,128]{2,1,0:T(8,128)S(1)} %pad_maximum_fusion.5), channel_id=1, source_target_pairs={{0,1},{1,2},{2,3},{3,4},{4,5},{5,6},{6,7},{7,8},{8,9},{9,10},{10,1... | collective-permute-start | bytes 1966088 | tf_op jit(solution)/shard_map/ppermute | solution.py:22
  4.7 19.0 %collective-permute-start.1 = (f32[20,64,128]{2,1,0:T(8,128)S(1)}, f32[20,64,128]{2,1,0:T(8,128)}, u32[]{:S(2)}, u32[]{:S(2)}) collective-permute-start(f32[20,64,128]{2,1,0:T(8,128)S(1)} %pad_maximum_fusion.5), channel_id=1, source_target_pairs={{1,0},{2,1},{3,2},{4,3},{5,4},{6,5},{7,6},{8,7},{9,8},{10,9},{11,1... | collective-permute-start | bytes 1966088 | tf_op jit(solution)/shard_map/ppermute | solution.py:24
  23.7 6.3 %collective-permute-done = f32[20,64,128]{2,1,0:T(8,128)S(1)} collective-permute-done((f32[20,64,128]{2,1,0:T(8,128)S(1)}, f32[20,64,128]{2,1,0:T(8,128)S(1)}, u32[]{:S(2)}, u32[]{:S(2)}) %collective-permute-start) | collective-permute-done | bytes 655392 | tf_op jit(solution)/shard_map/ppermute | solution.py:22
  30.0 0.0 copy-start.3
  30.0 0.9 copy-done.3
  30.9 0.9 collective-permute-done.1
  31.8 1.4 %fusion.95 = f32[20,64,384]{2,1,0:T(8,128)S(1)} fusion(f32[1,64,128]{2,1,0:T(8,128)S(1)} %fusion.99, f32[20,64,128]{2,1,0:T(8,128)} %collective-permute-done.1, f32[19,64,128]{2,1,0:T(8,128)S(1)} %pad_select_fusion.1, f32[20,64,128]{2,1,0:T(8,128)} %copy-done.3), kind=kLoop, calls=%fused_computation.238 | loop fusion | flops 1474560 | bytes 3932160 | tf_op jit(solution)/shard_map/concatenate | solution.py:20
  33.2 0.0 copy-start.4
  33.2 0.0 copy-start.5
  33.3 0.8 pad_maximum_fusion.6
  34.1 0.0 copy-done.4
  34.1 0.0 copy-done.5
  34.1 8.8 %conditional.2 = (f32[6,64,128]{2,1,0:T(8,128)S(1)}, f32[19,64,128]{2,1,0:T(8,128)S(1)}) conditional(s32[]{:T(128)} %convert_element_type.16, (f32[64,128]{1,0:T(8,128)S(1)}, f32[6,64,128]{2,1,0:T(8,128)S(1)}, s32[3,128]{1,0:T(4,128)S(1)}, f32[20,64,384]{2,1,0:T(8,128)S(1)}, f32[19,64,128]{2,1,0:T(8,128)S(1)}, ...), branch_computations={%region_0.2_spmd, %region_1.5_spmd} | conditional | flops 39255680 | bytes 34277588 | solution.py:141
  34.1 0.6 compare_and_fusion.5
  34.7 1.6 %copy.87 = f32[5,64,384]{1,0,2:T(8,128)S(1)} copy(f32[5,64,384]{2,1,0:T(8,128)} %get-tuple-element.156) | data formatting | bytes 983040 | tf_op jit(solution)/shard_map
  36.3 0.8 gather_fusion.1
  37.1 0.2 copy.78
  37.3 0.8 gather_fusion.2
  38.0 0.8 copy.79
  38.9 0.9 select_bitcast_fusion.3
  39.9 0.7 pad_clamp_fusion.5
  40.5 0.8 gather_fusion
  41.3 0.2 copy.77
  41.5 0.7 select_bitcast_fusion.5
  42.2 0.1 pad.27.clone
  42.3 0.1 fusion.26
  42.6 0.1 reduce_window_sum.12
  42.9 0.1 pad_select_fusion
  43.0 1.9 %collective-permute-start.3 = (f32[20,64,128]{2,1,0:T(8,128)S(1)}, f32[20,64,128]{2,1,0:T(8,128)S(1)}, u32[]{:S(2)}, u32[]{:S(2)}) collective-permute-start(f32[20,64,128]{2,1,0:T(8,128)S(1)} %pad_maximum_fusion.4), channel_id=1, source_target_pairs={{0,1},{1,2},{2,3},{3,4},{4,5},{5,6},{6,7},{7,8},{8,9},{9,10},{10,1... | collective-permute-start | bytes 1966088 | tf_op jit(solution)/shard_map/ppermute | solution.py:22
  44.9 13.5 %collective-permute-start.4 = (f32[20,64,128]{2,1,0:T(8,128)S(1)}, f32[20,64,128]{2,1,0:T(8,128)S(1)}, u32[]{:S(2)}, u32[]{:S(2)}) collective-permute-start(f32[20,64,128]{2,1,0:T(8,128)S(1)} %pad_maximum_fusion.4), channel_id=1, source_target_pairs={{1,0},{2,1},{3,2},{4,3},{5,4},{6,5},{7,6},{8,7},{9,8},{10,9},{11,1... | collective-permute-start | bytes 1966088 | tf_op jit(solution)/shard_map/ppermute | solution.py:24
  58.5 26.7 %collective-permute-start.2 = (f32[6,64,128]{2,1,0:T(8,128)S(1)}, f32[6,64,128]{2,1,0:T(8,128)S(1)}, u32[]{:S(2)}, u32[]{:S(2)}) collective-permute-start(f32[6,64,128]{2,1,0:T(8,128)S(1)} %get-tuple-element.81), channel_id=1, source_target_pairs={{0,512},{1,513},{2,514},{3,515},{4,516},{5,517},{6,518},{7,519},{8... | collective-permute-start | bytes 589832 | tf_op jit(solution)/shard_map/ppermute | solution.py:34
  85.2 1.3 %collective-permute-start.5 = (f32[64,128]{1,0:T(8,128)S(1)}, f32[64,128]{1,0:T(8,128)S(1)}, u32[]{:S(2)}, u32[]{:S(2)}) collective-permute-start(f32[64,128]{1,0:T(8,128)S(1)} %slice_bitcast_fusion.13), channel_id=1, source_target_pairs={{512,0},{513,1},{514,2},{515,3},{516,4},{517,5},{518,6},{519,7},{5... | collective-permute-start | bytes 98312 | tf_op jit(solution)/shard_map/ppermute | solution.py:34
  86.5 0.0 collective-permute-done.3
  86.5 0.0 collective-permute-done.4
  86.5 0.2 fusion.97
  86.7 0.8 pad_maximum_fusion.7
  87.6 1.0 collective-permute-done.2
  88.6 11.1 %collective-permute-done.5 = f32[64,128]{1,0:T(8,128)S(1)} collective-permute-done((f32[64,128]{1,0:T(8,128)S(1)}, f32[64,128]{1,0:T(8,128)S(1)}, u32[]{:S(2)}, u32[]{:S(2)}) %collective-permute-start.5) | collective-permute-done | bytes 32800 | tf_op jit(solution)/shard_map/ppermute | solution.py:34
  99.7 9.1 %conditional.3 = (f32[6,64,128]{2,1,0:T(8,128)S(1)}, f32[64,128]{1,0:T(8,128)S(1)}) conditional(s32[]{:T(128)} %convert_element_type.16, (f32[64,128]{1,0:T(8,128)S(1)}, f32[6,64,128]{2,1,0:T(8,128)S(1)}, s32[3,128]{1,0:T(4,128)S(1)}, f32[20,64,384]{2,1,0:T(8,128)S(1)}, f32[19,64,128]{2,1,0:T(8,128)S(1)}, /*index=5*/f32[19,19]{1,0:T(8,128)S(1)}, ...), branch_computations={%region_3.0_spmd, %region_4.8_spmd} | conditional | flops 38502016 | bytes 33763028 | solution.py:155
  99.8 1.6 %copy.89 = f32[5,64,384]{1,0,2:T(8,128)S(1)} copy(f32[5,64,384]{2,1,0:T(8,128)} %get-tuple-element.168) | data formatting | bytes 983040 | tf_op jit(solution)/shard_map
  101.4 0.8 gather_fusion.4
  102.1 0.8 copy.84
  103.0 0.8 gather_fusion.5
  103.8 0.8 copy.85
  104.6 1.0 select_bitcast_fusion.9
  105.6 0.0 copy-start.2
  105.7 0.6 copy-done.2
  106.3 0.8 gather_fusion.3
  107.1 0.2 copy.83
  107.3 0.1 pad.45.clone
  107.4 1.0 fusion.78
  108.6 0.1 reduce_window_sum.18
  108.9 0.6 select_bitcast_fusion.13
  109.5 0.7 select_bitcast_fusion.12
  (58 shorter events, 0.8 us)
Async XLA Ops:
  0.6 2.0 %copy-start.6 = (s32[128]{0:T(128)S(1)}, s32[128]{0:T(128)}, u32[]{:S(2)}) copy-start(s32[128]{0:T(128)} %param.16) | copy-start | bytes 1540
  2.8 27.2 %collective-permute-start = (f32[20,64,128]{2,1,0:T(8,128)S(1)}, f32[20,64,128]{2,1,0:T(8,128)S(1)}, u32[]{:S(2)}, u32[]{:S(2)}) collective-permute-start(f32[20,64,128]{2,1,0:T(8,128)S(1)} %pad_maximum_fusion.5), channel_id=1, source_target_pairs={{0,1},{1,2},{2,3},{3,4},{4,5},{5,6},{6,7},{7,8},{8,9},{9,10},{10,1... | collective-permute-start | bytes 1966088 | tf_op jit(solution)/shard_map/ppermute | solution.py:22
  4.7 27.0 %collective-permute-start.1 = (f32[20,64,128]{2,1,0:T(8,128)S(1)}, f32[20,64,128]{2,1,0:T(8,128)}, u32[]{:S(2)}, u32[]{:S(2)}) collective-permute-start(f32[20,64,128]{2,1,0:T(8,128)S(1)} %pad_maximum_fusion.5), channel_id=1, source_target_pairs={{1,0},{2,1},{3,2},{4,3},{5,4},{6,5},{7,6},{8,7},{9,8},{10,9},{11,1... | collective-permute-start | bytes 1966088 | tf_op jit(solution)/shard_map/ppermute | solution.py:24
  30.0 0.9 copy-start.3
  33.2 0.9 copy-start.4
  33.2 0.9 copy-start.5
  43.0 43.5 %collective-permute-start.3 = (f32[20,64,128]{2,1,0:T(8,128)S(1)}, f32[20,64,128]{2,1,0:T(8,128)S(1)}, u32[]{:S(2)}, u32[]{:S(2)}) collective-permute-start(f32[20,64,128]{2,1,0:T(8,128)S(1)} %pad_maximum_fusion.4), channel_id=1, source_target_pairs={{0,1},{1,2},{2,3},{3,4},{4,5},{5,6},{6,7},{7,8},{8,9},{9,10},{10,1... | collective-permute-start | bytes 1966088 | tf_op jit(solution)/shard_map/ppermute | solution.py:22
  44.9 41.6 %collective-permute-start.4 = (f32[20,64,128]{2,1,0:T(8,128)S(1)}, f32[20,64,128]{2,1,0:T(8,128)S(1)}, u32[]{:S(2)}, u32[]{:S(2)}) collective-permute-start(f32[20,64,128]{2,1,0:T(8,128)S(1)} %pad_maximum_fusion.4), channel_id=1, source_target_pairs={{1,0},{2,1},{3,2},{4,3},{5,4},{6,5},{7,6},{8,7},{9,8},{10,9},{11,1... | collective-permute-start | bytes 1966088 | tf_op jit(solution)/shard_map/ppermute | solution.py:24
  58.5 30.1 %collective-permute-start.2 = (f32[6,64,128]{2,1,0:T(8,128)S(1)}, f32[6,64,128]{2,1,0:T(8,128)S(1)}, u32[]{:S(2)}, u32[]{:S(2)}) collective-permute-start(f32[6,64,128]{2,1,0:T(8,128)S(1)} %get-tuple-element.81), channel_id=1, source_target_pairs={{0,512},{1,513},{2,514},{3,515},{4,516},{5,517},{6,518},{7,519},{8... | collective-permute-start | bytes 589832 | tf_op jit(solution)/shard_map/ppermute | solution.py:34
  85.2 14.5 %collective-permute-start.5 = (f32[64,128]{1,0:T(8,128)S(1)}, f32[64,128]{1,0:T(8,128)S(1)}, u32[]{:S(2)}, u32[]{:S(2)}) collective-permute-start(f32[64,128]{1,0:T(8,128)S(1)} %slice_bitcast_fusion.13), channel_id=1, source_target_pairs={{512,0},{513,1},{514,2},{515,3},{516,4},{517,5},{518,6},{519,7},{5... | collective-permute-start | bytes 98312 | tf_op jit(solution)/shard_map/ppermute | solution.py:34
  105.6 0.7 copy-start.2
where the time goes:
time: 112 us; the launch traced here: 110 us
  starting transfers between devices  64.3 us (57%)
  waiting for transfers between devices  19.3 us (17%)
  local copies, waits for them, and re-layouts  14.7 us (13%)
  other arithmetic  10.6 us (9%)
    ppermute x2, starting transfers between devices, padded(): lax.ppermute(head, axis, [((i + 1) % count, i) for i in range(count)])  32.5 us
    ppermute x2, starting transfers between devices, from_behind(): return lax.ppermute(block, axis, route)  28 us
    ppermute x2, waiting for transfers between devices, from_behind(): return lax.ppermute(block, axis, route)  12.2 us
    gather x12, local copies, waits for them, and re-layouts, transport(): remote = jnp.take(extended, neighbours[face_index], axis=2)  7.57 us
    ppermute x2, waiting for transfers between devices, padded(): lax.ppermute(tail, axis, [(i, (i + 1) % count) for i in range(count)])  6.31 us
    ppermute x2, starting transfers between devices, padded(): lax.ppermute(tail, axis, [(i, (i + 1) % count) for i in range(count)])  3.84 us
    another operation x4, local copies, waits for them, and re-layouts  3.22 us
    unnamed x10, local copies, waits for them, and re-layouts  2.92 us
  transfers between devices with their start and end apart: 6, of which 4 were waited for; matrix products, arithmetic and copies ran while one was open for 1% of the time, Pallas kernels for 0%

commit v1 on v0

v1 whole, which is shorter than its diff:
```python
import functools
import math

import jax
import jax.numpy as jnp
from jax import lax
from jax.experimental import pallas as pl
from jax.experimental.pallas import tpu as pltpu
from jax.sharding import PartitionSpec as P

MESH = pl.DeviceIdType.MESH

NT = 19
LEV = 64
COL = 128
LB = 8
NB = LEV // LB
PAD = 8

ROTATE_COS = math.cos(0.3)
ROTATE_SIN = math.sin(0.3)


def rows(block, shift=0):
    if isinstance(block, int):
        return pl.ds(PAD + LB * block + shift, LB)
    start = pl.multiple_of(block * LB, LB)
    return pl.ds(start + (PAD + shift), LB)


def levels(block):
    return pl.ds(pl.multiple_of(block * LB, LB), LB)


def level_index(block):
    return lax.broadcasted_iota(jnp.int32, (LB, COL), 0) + block * LB


def lane_take(values, index):
    return jnp.take_along_axis(values, index, axis=1, mode="promise_in_bounds")


def light(chl, top):
    absorbed = 0.01 + 0.3 * jax.nn.softplus(chl)
    above = (
        lax.broadcasted_iota(jnp.int32, (LEV, LEV), 1)
        < lax.broadcasted_iota(jnp.int32, (LEV, LEV), 0)
    ).astype(jnp.float32)
    depth = jnp.dot(
        above, absorbed, precision=lax.Precision.HIGHEST, preferred_element_type=jnp.float32
    )
    ceiling = jnp.exp(-depth)
    bottom = jnp.exp(-(depth + absorbed))
    return top * ceiling, 4.0 * top * (ceiling - bottom)


def kernel(
    n, ocean_hbm, tracer_hbm, reaction, wet_in, near_in, ocean_out, chl_out,
    fields, own, left_in, right_in, one, left_one, right_one,
    moved, link, lag, sun, shade, heat, chl_got, wet_left, wet_right,
    load_sem, halo_send, halo_recv, wet_send, wet_recv, comp_send, comp_recv, sun_send, sun_recv,
):
    comp = lax.axis_index("comp")
    tile = lax.axis_index("tile")
    right = lax.rem(tile + 1, n)
    left = lax.rem(tile + n - 1, n)
    to_right, to_left, partner = (comp, right), (comp, left), (1 - comp, tile)
    is_ocean = comp == 0

    def remote(src, dst, send, recv, device):
        return pltpu.make_async_remote_copy(
            src_ref=src, dst_ref=dst, send_sem=send, recv_sem=recv,
            device_id=device, device_id_type=MESH,
        )

    load_fields = pltpu.make_async_copy(ocean_hbm, fields, load_sem.at[0])
    load_own = pltpu.make_async_copy(tracer_hbm, own, load_sem.at[1])
    load_fields.start()
    load_own.start()

    barrier = pltpu.get_barrier_semaphore()
    for device in (to_left, to_right, partner):
        pl.semaphore_signal(barrier, inc=1, device_id=device, device_id_type=MESH)
    pl.semaphore_wait(barrier, 3)

    def wet_copies():
        return (
            remote(wet_in, wet_left, wet_send.at[0], wet_recv.at[0], to_right),
            remote(wet_in, wet_right, wet_send.at[1], wet_recv.at[1], to_left),
        )

    def first_halo(b, count):
        source = ocean_hbm if count < NT else tracer_hbm
        source = source.at[pl.ds(0, count), levels(b)]
        at = (b, pl.ds(0, count))
        return (
            remote(source, left_in.at[at], halo_send.at[0, 0, b], halo_recv.at[0, 0, b], to_right),
            remote(source, right_in.at[at], halo_send.at[0, 1, b], halo_recv.at[0, 1, b], to_left),
        )

    def second_halo(b, count):
        source = lag.at[:, rows(b)] if count < NT else one.at[b]
        at = (b, pl.ds(0, count))
        return (
            remote(source, left_one.at[at], halo_send.at[1, 0, b], halo_recv.at[1, 0, b], to_right),
            remote(source, right_one.at[at], halo_send.at[1, 1, b], halo_recv.at[1, 1, b], to_left),
        )

    def lag_copy(b):
        at = (slice(None), rows(b))
        return remote(lag.at[at], lag.at[at], comp_send.at[b], comp_recv.at[b], partner)

    def chl_copy(b):
        return remote(one.at[b, 0], chl_got.at[levels(b)], comp_send.at[b], comp_recv.at[b], partner)

    def sun_copy():
        return remote(ocean_hbm.at[5, pl.ds(0, LB)], sun, sun_send, sun_recv, partner)

    for copy in wet_copies():
        copy.start()

    def each(body):
        lax.fori_loop(0, NB, lambda b, c: (body(b), c)[1], 0)

    def start_first(count):
        def body(b):
            for copy in first_halo(b, count):
                copy.start()

        each(body)

    @pl.when(is_ocean)
    def _():
        sun_copy().start()
        start_first(4)

    @pl.when(jnp.logical_not(is_ocean))
    def _():
        start_first(NT)

    zero = jnp.zeros((PAD, COL), jnp.float32)
    link[pl.ds(0, PAD)] = zero
    for i in range(4):
        lag[i, pl.ds(0, PAD)] = zero
        lag[i, pl.ds(PAD + LEV, PAD)] = zero
    for i in range(NT):
        moved[i, pl.ds(0, PAD)] = zero
        moved[i, pl.ds(PAD + LEV, PAD)] = zero

    wet = jnp.broadcast_to(wet_in[...], (LB, COL))
    near = [jnp.broadcast_to(near_in[pl.ds(k, 1), :], (LB, COL)) for k in range(3)]
    index = [jnp.bitwise_and(p, COL - 1) for p in near]
    in_left = [p < COL for p in near]
    in_right = [p >= 2 * COL for p in near]

    def reach(k, at_left, at_own, at_right):
        inner = jnp.where(in_right[k], lane_take(at_right, index[k]), lane_take(at_own, index[k]))
        return jnp.where(in_left[k], lane_take(at_left, index[k]), inner)

    for copy in wet_copies():
        copy.wait_recv()
    wet_l = jnp.broadcast_to(wet_left[...], (LB, COL))
    wet_r = jnp.broadcast_to(wet_right[...], (LB, COL))
    wet_near = [jnp.minimum(reach(k, wet_l, wet, wet_r), wet) for k in range(3)]

    def face_weights(b, east, north):
        level = level_index(b)
        found = []
        for k in range(3):
            angle = 2.0 * math.pi * k / 3.0
            w = 0.05 + 0.25 * jax.nn.sigmoid(east * math.cos(angle) + north * math.sin(angle))
            found.append(jnp.where(level < wet_near[k], w, 0.0))
        return found

    def move(weights, stay, at_left, at_own, at_right):
        total = stay * at_own
        for k in range(3):
            total = total + weights[k] * reach(k, at_left, at_own, at_right)
        return total

    def stir(b, mixing):
        below = jnp.where(level_index(b) + 1 < wet, 0.02 + 0.13 * jax.nn.sigmoid(mixing), 0.0)
        link[rows(b)] = below
        above = link[rows(b, -1)]
        return 1.0 - below - above, below, above

    def stirred(i, b, weights):
        return (
            weights[0] * moved[i, rows(b)]
            + weights[1] * moved[i, rows(b, 1)]
            + weights[2] * moved[i, rows(b, -1)]
        )

    def staged(first, second):
        def body(b, carry):
            @pl.when(b < NB)
            def _():
                first(b)

            @pl.when(b > 0)
            def _():
                second(b - 1)

            return carry

        lax.fori_loop(0, NB + 1, body, 0)

    def move_ocean(b, state, at_left, at_right):
        weights = face_weights(b, state[2], state[3])
        steady = [jnp.where(level_index(b) < wet_near[k], 0.15, 0.0) for k in range(3)]
        q = []
        for i in range(4):
            w = weights if i < 2 else steady
            q.append(move(w, 1.0 - w[0] - w[1] - w[2], at_left[b, i], state[i], at_right[b, i]))
        moved[0, rows(b)] = q[0]
        moved[1, rows(b)] = q[1]
        moved[2, rows(b)] = ROTATE_COS * q[2] + ROTATE_SIN * q[3]
        moved[3, rows(b)] = ROTATE_COS * q[3] - ROTATE_SIN * q[2]

    def lag_mixing(b):
        return lag[0, rows(b)] - lag[0, rows(b, 1)]

    @pl.when(is_ocean)
    def _():
        load_fields.wait()
        load_own.wait()
        top = fields[5, pl.ds(0, 1)]
        shade_now, heat_now = light(own[0], top)
        heat[...] = heat_now

        def first_move(b):
            for copy in first_halo(b, 4):
                copy.wait_recv()
            move_ocean(b, [fields[i, levels(b)] for i in range(4)], left_in, right_in)

        def first_stir(b):
            act = level_index(b) < wet
            weights = stir(b, fields[4, levels(b)])
            lag[0, rows(b)] = stirred(0, b, weights) + heat[levels(b)]
            for i in range(1, 4):
                lag[i, rows(b)] = jnp.where(act, stirred(i, b, weights), 0.0)
            lag_copy(b).start()
            for copy in second_halo(b, 4):
                copy.start()

        staged(first_move, first_stir)

        def second_move(b):
            for copy in second_halo(b, 4):
                copy.wait_recv()
            warm = jnp.where(level_index(b) < wet, lag[0, rows(b)], 0.0)
            move_ocean(b, [warm] + [lag[i, rows(b)] for i in range(1, 4)], left_one, right_one)

        def second_stir(b):
            act = level_index(b) < wet
            weights = stir(b, jnp.where(act, lag_mixing(b), 0.0))
            shade[rows(b)] = stirred(0, b, weights)
            for i in range(1, 4):
                ocean_out[i, levels(b)] = jnp.where(act, stirred(i, b, weights), 0.0)

        staged(second_move, second_stir)

        def got(b):
            chl_copy(b).wait_recv()

        each(got)
        chl = chl_got[...]
        chl_out[...] = chl
        top_two = jnp.where(wet_in[...] > 0, top, 0.0)
        shade_two, heat_two = light(chl, top_two)
        warm = shade[pl.ds(PAD, LEV)] + heat_two
        shade[pl.ds(PAD, LEV)] = warm
        below = shade[pl.ds(PAD + 1, LEV)]
        level = lax.broadcasted_iota(jnp.int32, (LEV, COL), 0)
        act = level < wet_in[...]
        ocean_out[0] = jnp.where(act, warm, 0.0)
        ocean_out[4] = jnp.where(jnp.logical_and(act, level < LEV - 1), warm - below, 0.0)
        ocean_out[5] = jnp.where(act, shade_two, 0.0)

    @pl.when(jnp.logical_not(is_ocean))
    def _():
        load_fields.wait()
        load_own.wait()

        def first_move(b):
            weights = face_weights(b, fields[2, levels(b)], fields[3, levels(b)])
            stay = 1.0 - weights[0] - weights[1] - weights[2]
            for copy in first_halo(b, NT):
                copy.wait_recv()
            for i in range(NT):
                moved[i, rows(b)] = move(weights, stay, left_in[b, i], own[i, levels(b)], right_in[b, i])

        def first_stir(b):
            act = level_index(b) < wet
            weights = stir(b, fields[4, levels(b)])
            warm = fields[0, levels(b)] + 0.5 * fields[1, levels(b)]
            rate = 0.5 * fields[5, levels(b)] * jax.nn.sigmoid(warm)
            bent = []
            for i in range(NT):
                y = stirred(i, b, weights)
                one[b, i] = y
                bent.append(jnp.tanh(y))
            for i in range(NT):
                growth = reaction[i, 0] * bent[0]
                for j in range(1, NT):
                    growth = growth + reaction[i, j] * bent[j]
                one[b, i] = jnp.where(act, one[b, i] + rate * growth, 0.0)
            for copy in second_halo(b, NT):
                copy.start()
            chl_copy(b).start()

        staged(first_move, first_stir)

        sun_copy().wait_recv()
        shade_now, _ = light(own[0], sun[pl.ds(0, 1)])
        shade[pl.ds(PAD, LEV)] = shade_now

        def second_move(b):
            lag_copy(b).wait_recv()
            weights = face_weights(b, lag[2, rows(b)], lag[3, rows(b)])
            stay = 1.0 - weights[0] - weights[1] - weights[2]
            for copy in second_halo(b, NT):
                copy.wait_recv()
            for i in range(NT):
                moved[i, rows(b)] = move(weights, stay, left_one[b, i], one[b, i], right_one[b, i])

        def second_stir(b):
            level = level_index(b)
            act = level < wet
            mixing = jnp.where(jnp.logical_and(act, level < LEV - 1), lag_mixing(b), 0.0)
            weights = stir(b, mixing)
            warm = jnp.where(act, lag[0, rows(b)], 0.0)
            sunlight = jnp.where(act, shade[rows(b)], 0.0)
            ocean_out[0, levels(b)] = warm
            for i in range(1, 4):
                ocean_out[i, levels(b)] = lag[i, rows(b)]
            ocean_out[4, levels(b)] = mixing
            ocean_out[5, levels(b)] = sunlight
            rate = 0.5 * sunlight * jax.nn.sigmoid(warm + 0.5 * lag[1, rows(b)])
            chl = stirred(0, b, weights)
            growth = reaction[0, 0] * jnp.tanh(chl)
            for j in range(1, NT):
                growth = growth + reaction[0, j] * jnp.tanh(stirred(j, b, weights))
            chl_out[levels(b)] = jnp.where(act, chl + rate * growth, 0.0)

        staged(second_move, second_stir)

    for copy in wet_copies():
        copy.wait_send()

    def drain(count):
        def body(b):
            for copy in first_halo(b, count) + second_halo(b, count):
                copy.wait_send()
            (lag_copy if count < NT else chl_copy)(b).wait_send()

        each(body)

    @pl.when(is_ocean)
    def _():
        sun_copy().wait_send()
        drain(4)

    @pl.when(jnp.logical_not(is_ocean))
    def _():
        drain(NT)


def per_device(ocean_fields, tracers, reaction, wet_levels, neighbours):
    f32, vmem = jnp.float32, pltpu.VMEM
    in_vmem = pl.BlockSpec(memory_space=vmem)
    in_hbm = pl.BlockSpec(memory_space=pl.ANY)
    dma = pltpu.SemaphoreType.DMA
    ocean_out, chl_out = pl.pallas_call(
        functools.partial(kernel, lax.axis_size("tile")),
        out_shape=(
            jax.ShapeDtypeStruct((6, LEV, COL), f32),
            jax.ShapeDtypeStruct((LEV, COL), f32),
        ),
        in_specs=[in_hbm, in_hbm, pl.BlockSpec(memory_space=pltpu.SMEM), in_vmem, in_vmem],
        out_specs=(in_vmem, in_vmem),
        scratch_shapes=[
            vmem((6, LEV, COL), f32),
            vmem((NT, LEV, COL), f32),
            vmem((NB, NT, LB, COL), f32),
            vmem((NB, NT, LB, COL), f32),
            vmem((NB, NT, LB, COL), f32),
            vmem((NB, NT, LB, COL), f32),
            vmem((NB, NT, LB, COL), f32),
            vmem((NT, LEV + 2 * PAD, COL), f32),
            vmem((LEV + 2 * PAD, COL), f32),
            vmem((4, LEV + 2 * PAD, COL), f32),
            vmem((LB, COL), f32),
            vmem((LEV + 2 * PAD, COL), f32),
            vmem((LEV, COL), f32),
            vmem((LEV, COL), f32),
            vmem((1, COL), jnp.int32),
            vmem((1, COL), jnp.int32),
            dma((2,)),
            dma((2, 2, NB)),
            dma((2, 2, NB)),
            dma((2,)),
            dma((2,)),
            dma((NB,)),
            dma((NB,)),
            dma,
            dma,
        ],
        compiler_params=pltpu.CompilerParams(
            collective_id=0, has_side_effects=True, vmem_limit_bytes=32 * 2**20
        ),
    )(ocean_fields[0], tracers, reaction, wet_levels[None, :], neighbours)
    return ocean_out[None], chl_out[None]


def solution(mesh):
    return jax.shard_map(
        per_device,
        mesh=mesh,
        in_specs=(
            P("comp", None, None, "tile"),
            P(None, None, "tile"),
            P(),
            P("tile"),
            P(None, "tile"),
        ),
        out_specs=(P("comp", None, None, "tile"), P("comp", None, "tile")),
        check_vma=False,
    )
```

time: 112 us -> 59.6 us (0.53); the launches traced: 110 us -> 59.4 us
  starting transfers between devices: 64.3 us -> 0 us
  Pallas kernels: 0 us -> 54 us
  waiting for transfers between devices: 19.3 us -> 0 us
  other arithmetic: 10.6 us -> 0 us
  local copies, waits for them, and re-layouts: 14.7 us -> 4.67 us
    ppermute x6 -> x0, starting transfers between devices: 64.3 us -> none  [the longest x2 32.5 us: padded(): lax.ppermute(head, axis, [((i + 1) % count, i) for i in range(count)])]
    pallas_call x0 -> x1, Pallas kernels: none -> 54 us  [per_device(): pl.pallas_call(functools.partial(kernel, lax.axis_size('tile')), out_shap...]
    ppermute x6 -> x0, waiting for transfers between devices: 19.3 us -> none  [the longest x2 12.2 us: from_behind(): return lax.ppermute(block, axis, route)]
    gather x12 -> x0, local copies, waits for them, and re-layouts: 7.57 us -> none  [transport(): remote = jnp.take(extended, neighbours[face_index], axis=2)]
    another operation x6 -> x0, local copies, waits for them, and re-layouts: 3.37 us -> none
    concatenate x6 -> x0, other arithmetic: 3.31 us -> none  [the longest x2 1.64 us: step_rims(): ocean_ext = jnp.concatenate([extended[:4], extended[tracer_rows:]], axis=0)]
    select_n x6 -> x0, other arithmetic: 2.74 us -> none  [the longest x4 2.63 us: transport(): remote = jnp.take(extended, neighbours[face_index], axis=2)]
    unnamed x10 -> x12, local copies, waits for them, and re-layouts: 2.92 us -> 4.67 us
  transfers between devices with their start and end apart: 6 -> 0, of which waited for: 4 -> 0; matrix products, arithmetic and copies ran while one was open for 1% -> 0% of each run, Pallas kernels for 0% -> 0%
where the time goes in v1:
time: 59.6 us; the launch traced here: 59.4 us
  Pallas kernels  54 us (91%)
  local copies, waits for them, and re-layouts  4.67 us (8%)
  between operations  0.66 us (1%)
    pallas_call x1, Pallas kernels, per_device(): pl.pallas_call(functools.partial(kernel, lax.axis_size('tile')), out_shap...  54 us
    unnamed x12, local copies, waits for them, and re-layouts  4.67 us

profile of v1, /device:TPU:6, one launch (start us, length us, event | category | flops | bytes accessed | tf_op | source)
XLA Modules:
  0.0 59.4 jit_solution(8718966268718021274)
XLA Ops:
  0.6 0.0 copy-start.3
  0.6 0.0 copy-start.4
  0.7 0.7 %copy-done.3 = s32[3,128]{1,0:T(4,128)S(1)} copy-done((s32[3,128]{1,0:T(4,128)S(1)}, s32[3,128]{1,0:T(4,128)}, u32[]{:S(2)}) %copy-start.3) | copy-done | bytes 1560
  1.3 0.0 copy-done.4
  1.3 0.0 copy-start
  1.3 1.1 %copy-done = f32[19,64,128]{2,1,0:T(8,128)S(1)} copy-done((f32[19,64,128]{2,1,0:T(8,128)S(1)}, f32[19,64,128]{2,1,0:T(8,128)}, u32[]{:S(2)}) %copy-start) | copy-done | bytes 622616
  2.4 0.0 copy-start.1
  2.4 0.9 %copy-done.1 = f32[1,6,64,128]{3,2,1,0:T(8,128)S(1)} copy-done((f32[1,6,64,128]{3,2,1,0:T(8,128)S(1)}, f32[1,6,64,128]{3,2,1,0:T(8,128)}, u32[]{:S(2)}) %copy-start.1) | copy-done | bytes 196632
  3.3 0.0 copy-start.2
  3.3 0.7 %copy-done.2 = f32[19,19]{1,0:T(8,128)S(1)} copy-done((f32[19,19]{1,0:T(8,128)S(1)}, f32[19,19]{1,0:T(8,128)}, u32[]{:S(2)}) %copy-start.2) | copy-done | bytes 1468
  4.0 54.0 %shard_map.68 = (f32[6,64,128]{2,1,0:T(8,128)S(1)}, f32[64,128]{1,0:T(8,128)S(1)}) custom-call(f32[6,64,128]{2,1,0:T(8,128)S(1)} %bitcast.5, f32[19,64,128]{2,1,0:T(8,128)S(1)} %copy-done, f32[19,19]{1,0:T(8,128)S(1)} %copy-done.2, s32[1,128]{1,0:T(1,128)S(1)} %bitcast.7, s32[3,128]{1,0:T(4,128)S(1)} %copy-done.3), custom_call_target="tpu_custom_call" | custom-call | tf_op jit(solution)/shard_map/pallas_call | solution.py:374
  58.1 0.7 %copy.9 = f32[1,6,64,128]{3,2,1,0:T(8,128)} copy(f32[1,6,64,128]{3,2,1,0:T(8,128)S(1)} %bitcast.4) | data formatting | bytes 393216
  58.7 0.6 %copy.10 = f32[1,64,128]{2,1,0:T(8,128)} copy(f32[1,64,128]{2,1,0:T(8,128)S(1)} %bitcast.6) | data formatting | bytes 65536
Async XLA Ops:
  0.6 0.7 %copy-start.3 = (s32[3,128]{1,0:T(4,128)S(1)}, s32[3,128]{1,0:T(4,128)}, u32[]{:S(2)}) copy-start(s32[3,128]{1,0:T(4,128)} %near_in.1) | copy-start | bytes 4612
  0.6 0.7 %copy-start.4 = (s32[128]{0:T(128)S(1)}, s32[128]{0:T(128)}, u32[]{:S(2)}) copy-start(s32[128]{0:T(128)} %param.8) | copy-start | bytes 1540
  1.3 1.1 %copy-start = (f32[19,64,128]{2,1,0:T(8,128)S(1)}, f32[19,64,128]{2,1,0:T(8,128)}, u32[]{:S(2)}) copy-start(f32[19,64,128]{2,1,0:T(8,128)} %tracer_hbm.1) | copy-start | bytes 1867780
  2.4 0.9 %copy-start.1 = (f32[1,6,64,128]{3,2,1,0:T(8,128)S(1)}, f32[1,6,64,128]{3,2,1,0:T(8,128)}, u32[]{:S(2)}) copy-start(f32[1,6,64,128]{3,2,1,0:T(8,128)} %param.5) | copy-start | bytes 589828
  3.3 0.7 %copy-start.2 = (f32[19,19]{1,0:T(8,128)S(1)}, f32[19,19]{1,0:T(8,128)}, u32[]{:S(2)}) copy-start(f32[19,19]{1,0:T(8,128)} %reaction.1) | copy-start | bytes 4336

commit v2 on v1

v2 whole, which is shorter than its diff:
```python
import functools
import math

import jax
import jax.numpy as jnp
from jax import lax
from jax.experimental import pallas as pl
from jax.experimental.pallas import tpu as pltpu
from jax.sharding import PartitionSpec as P

MESH = pl.DeviceIdType.MESH

NT = 19
LEV = 64
COL = 128
LB = 8
NB = LEV // LB
PAD = 8

TURN = 128
SPAN = 16
DEPTH = 8
EARLY = 4

ROTATE_COS = math.cos(0.3)
ROTATE_SIN = math.sin(0.3)


def rows(block, shift=0):
    if isinstance(block, int):
        return pl.ds(PAD + LB * block + shift, LB)
    start = pl.multiple_of(block * LB, LB)
    return pl.ds(start + (PAD + shift), LB)


def levels(block):
    return pl.ds(pl.multiple_of(block * LB, LB), LB)


def level_index(block):
    return lax.broadcasted_iota(jnp.int32, (LB, COL), 0) + block * LB


def lane_take(values, index):
    return jnp.take_along_axis(values, index, axis=1, mode="promise_in_bounds")


def light(chl, top):
    absorbed = 0.01 + 0.3 * jax.nn.softplus(chl)
    above = (
        lax.broadcasted_iota(jnp.int32, (LEV, LEV), 1)
        < lax.broadcasted_iota(jnp.int32, (LEV, LEV), 0)
    ).astype(jnp.float32)
    depth = jnp.dot(
        above, absorbed, precision=lax.Precision.HIGHEST, preferred_element_type=jnp.float32
    )
    ceiling = jnp.exp(-depth)
    bottom = jnp.exp(-(depth + absorbed))
    return top * ceiling, 4.0 * top * (ceiling - bottom)


def kernel(
    n, ocean_hbm, tracer_hbm, reaction_hbm, wet_hbm, near_hbm, ocean_out, chl_out,
    fields, own, left_field, right_field, left_in, right_in, one, left_one, right_one,
    moved, link, lag, sun, shade, heat, given, chl_got, wet_in, near_in, wet_left, wet_right,
    reaction, load_sem, halo_send, halo_recv, wet_send, wet_recv, comp_send, comp_recv,
    given_send, given_recv, sun_send, sun_recv, cross_send, cross_wet_send,
    ready_partner, ready_turn, ready_cross,
):
    turn = min(TURN, n)
    comp = lax.axis_index("comp")
    tile = lax.axis_index("tile")
    right = lax.rem(tile + 1, n)
    left = lax.rem(tile + n - 1, n)
    to_right, to_left, partner = (comp, right), (comp, left), (1 - comp, tile)
    is_ocean = comp == 0
    is_bgc = jnp.logical_not(is_ocean)
    place = lax.rem(tile, turn)
    first, last = place == 0, place == turn - 1
    not_first, not_last = jnp.logical_not(first), jnp.logical_not(last)

    def is_early(t):
        return lax.rem(lax.div(t, SPAN), DEPTH) < EARLY

    early = is_early(tile)
    late = jnp.logical_not(early)

    def remote(src, dst, send, recv, device):
        return pltpu.make_async_remote_copy(
            src_ref=src, dst_ref=dst, send_sem=send, recv_sem=recv,
            device_id=device, device_id_type=MESH,
        )

    def signal(semaphore, device):
        pl.semaphore_signal(semaphore, inc=1, device_id=device, device_id_type=MESH)

    def when(*conditions):
        return pl.when(functools.reduce(jnp.logical_and, conditions))

    loads = [
        pltpu.make_async_copy(src, dst, load_sem.at[i])
        for i, (src, dst) in enumerate(
            (
                (wet_hbm, wet_in),
                (near_hbm, near_in),
                (ocean_hbm, fields),
                (tracer_hbm, own),
                (reaction_hbm, reaction),
            )
        )
    ]
    for copy in loads:
        copy.start()

    barrier = pltpu.get_barrier_semaphore()
    signal(barrier, to_left)

    @pl.when(not_last)
    def _():
        signal(barrier, to_right)

    @pl.when(is_ocean)
    def _():
        signal(barrier, partner)

        @pl.when(last)
        def _():
            signal(barrier, (1, right))

        @pl.when(first)
        def _():
            signal(barrier, (1, left))

    turned = jnp.logical_or(first, last).astype(jnp.int32)
    pl.semaphore_wait(barrier, 2 - first.astype(jnp.int32) + comp * (1 + turned))

    @pl.when(last)
    def _():
        signal(ready_turn, to_right)

    @pl.when(is_bgc)
    def _():
        signal(ready_partner, partner)

        @pl.when(first)
        def _():
            signal(ready_cross, (0, left))

        @pl.when(last)
        def _():
            signal(ready_cross, (0, right))

    def wet_right_copy():
        return remote(wet_in, wet_left, wet_send.at[0], wet_recv.at[0], to_right)

    def wet_left_copy():
        return remote(wet_in, wet_right, wet_send.at[1], wet_recv.at[1], to_left)

    def tracer_right(b, device=to_right, send=None):
        send = halo_send.at[0, 0, b] if send is None else send
        return remote(tracer_hbm.at[:, levels(b)], left_in.at[b], send, halo_recv.at[0, 0, b], device)

    def tracer_left(b, device=to_left, send=None):
        send = halo_send.at[0, 1, b] if send is None else send
        return remote(tracer_hbm.at[:, levels(b)], right_in.at[b], send, halo_recv.at[0, 1, b], device)

    def field_right(b):
        source = ocean_hbm.at[pl.ds(0, 4), levels(b)]
        return remote(source, left_field.at[b], halo_send.at[2, 0, b], halo_recv.at[2, 0, b], to_right)

    def field_left(b):
        source = ocean_hbm.at[pl.ds(0, 4), levels(b)]
        return remote(source, right_field.at[b], halo_send.at[2, 1, b], halo_recv.at[2, 1, b], to_left)

    def second_halo(b, count):
        source = lag.at[:, rows(b)] if count < NT else one.at[b]
        at = (b, pl.ds(0, count))
        return (
            remote(source, left_one.at[at], halo_send.at[1, 0, b], halo_recv.at[1, 0, b], to_right),
            remote(source, right_one.at[at], halo_send.at[1, 1, b], halo_recv.at[1, 1, b], to_left),
        )

    def lag_copy(b):
        at = (slice(None), rows(b))
        return remote(lag.at[at], lag.at[at], comp_send.at[b], comp_recv.at[b], partner)

    def chl_copy(b):
        return remote(one.at[b, 0], chl_got.at[levels(b)], comp_send.at[b], comp_recv.at[b], partner)

    def given_copy(b):
        source = fields.at[pl.ds(2, 4), levels(b)]
        return remote(source, given.at[:, levels(b)], given_send.at[b], given_recv.at[b], partner)

    def sun_copy():
        return remote(ocean_hbm.at[5, pl.ds(0, LB)], sun, sun_send, sun_recv, partner)

    def cross_wet():
        if_last = remote(wet_in, wet_left, cross_wet_send, wet_recv.at[0], (1, right))
        if_first = remote(wet_in, wet_right, cross_wet_send, wet_recv.at[1], (1, left))
        return if_last, if_first

    def cross_tracer(b):
        return (
            tracer_right(b, (1, right), cross_send.at[b]),
            tracer_left(b, (1, left), cross_send.at[b]),
        )

    def each(body):
        lax.fori_loop(0, NB, lambda b, c: (body(b), c)[1], 0)

    def run(copies, method):
        each(lambda b: getattr(copies(b), method)())

    def ready_wait(semaphore):
        pl.semaphore_wait(semaphore, 1)

    loads[0].wait()

    @pl.when(is_ocean)
    def _():
        wet_right_copy().start()
        run(field_right, "start")

        @pl.when(first)
        def _():
            ready_wait(ready_turn)

        wet_left_copy().start()
        run(field_left, "start")

        @pl.when(is_early(right))
        def _():
            run(tracer_right, "start")

        @pl.when(is_early(left))
        def _():
            run(tracer_left, "start")

    @pl.when(is_bgc)
    def _():
        @pl.when(not_last)
        def _():
            wet_right_copy().start()

        @pl.when(not_first)
        def _():
            wet_left_copy().start()

        def start_both(b):
            @pl.when(not_last)
            def _():
                tracer_right(b).start()

            @pl.when(not_first)
            def _():
                tracer_left(b).start()

        each(start_both)

    @when(is_ocean, last)
    def _():
        ready_wait(ready_cross)
        cross_wet()[0].start()
        run(lambda b: cross_tracer(b)[0], "start")

    zero = jnp.zeros((PAD, COL), jnp.float32)
    link[pl.ds(0, PAD)] = zero
    for i in range(4):
        lag[i, pl.ds(0, PAD)] = zero
        lag[i, pl.ds(PAD + LEV, PAD)] = zero
    for i in range(NT):
        moved[i, pl.ds(0, PAD)] = zero
        moved[i, pl.ds(PAD + LEV, PAD)] = zero

    for copy in loads[1:]:
        copy.wait()

    def growth_rate(b):
        warm = fields[0, levels(b)] + 0.5 * fields[1, levels(b)]
        return 0.5 * fields[5, levels(b)] * jax.nn.sigmoid(warm)

    @pl.when(is_bgc)
    def _():
        def rate(b):
            fields[5, levels(b)] = growth_rate(b)

            @pl.when(early)
            def _():
                given_copy(b).start()

        each(rate)

    wet = jnp.broadcast_to(wet_in[...], (LB, COL))
    near = [jnp.broadcast_to(near_in[pl.ds(k, 1), :], (LB, COL)) for k in range(3)]
    index = [jnp.bitwise_and(p, COL - 1) for p in near]
    in_left = [p < COL for p in near]
    in_right = [p >= 2 * COL for p in near]

    def reach(k, at_left, at_own, at_right):
        inner = jnp.where(in_right[k], lane_take(at_right, index[k]), lane_take(at_own, index[k]))
        return jnp.where(in_left[k], lane_take(at_left, index[k]), inner)

    wet_right_copy().wait_recv()
    wet_left_copy().wait_recv()
    wet_l = jnp.broadcast_to(wet_left[...], (LB, COL))
    wet_r = jnp.broadcast_to(wet_right[...], (LB, COL))
    wet_near = [jnp.minimum(reach(k, wet_l, wet, wet_r), wet) for k in range(3)]

    def face_weights(b, east, north):
        level = level_index(b)
        found = []
        for k in range(3):
            angle = 2.0 * math.pi * k / 3.0
            w = 0.05 + 0.25 * jax.nn.sigmoid(east * math.cos(angle) + north * math.sin(angle))
            found.append(jnp.where(level < wet_near[k], w, 0.0))
        return found

    def move(weights, stay, at_left, at_own, at_right):
        total = stay * at_own
        for k in range(3):
            total = total + weights[k] * reach(k, at_left, at_own, at_right)
        return total

    def stir(b, mixing):
        below = jnp.where(level_index(b) + 1 < wet, 0.02 + 0.13 * jax.nn.sigmoid(mixing), 0.0)
        link[rows(b)] = below
        above = link[rows(b, -1)]
        return 1.0 - below - above, below, above

    def stirred(i, b, weights):
        return (
            weights[0] * moved[i, rows(b)]
            + weights[1] * moved[i, rows(b, 1)]
            + weights[2] * moved[i, rows(b, -1)]
        )

    def staged(ahead, behind):
        def body(b, carry):
            @pl.when(b < NB)
            def _():
                ahead(b)

            @pl.when(b > 0)
            def _():
                behind(b - 1)

            return carry

        lax.fori_loop(0, NB + 1, body, 0)

    def move_ocean(b, state, at_left, at_right):
        weights = face_weights(b, state[2], state[3])
        steady = [jnp.where(level_index(b) < wet_near[k], 0.15, 0.0) for k in range(3)]
        q = []
        for i in range(4):
            w = weights if i < 2 else steady
            q.append(move(w, 1.0 - w[0] - w[1] - w[2], at_left[b, i], state[i], at_right[b, i]))
        moved[0, rows(b)] = q[0]
        moved[1, rows(b)] = q[1]
        moved[2, rows(b)] = ROTATE_COS * q[2] + ROTATE_SIN * q[3]
        moved[3, rows(b)] = ROTATE_COS * q[3] - ROTATE_SIN * q[2]

    def move_tracers(b, east, north, at_left, at_own, at_right):
        weights = face_weights(b, east, north)
        stay = 1.0 - weights[0] - weights[1] - weights[2]
        for i in range(NT):
            moved[i, rows(b)] = move(weights, stay, at_left[b, i], at_own(i), at_right[b, i])

    def first_halo_wait(b):
        tracer_right(b).wait_recv()
        tracer_left(b).wait_recv()

    def second_halo_wait(b, count):
        for copy in second_halo(b, count):
            copy.wait_recv()

    def chl_after(b, weights, rate):
        chl = stirred(0, b, weights)
        growth = reaction[0, 0] * jnp.tanh(chl)
        for j in range(1, NT):
            growth = growth + reaction[0, j] * jnp.tanh(stirred(j, b, weights))
        return jnp.where(level_index(b) < wet, chl + rate * growth, 0.0)

    def lag_mixing(b):
        return lag[0, rows(b)] - lag[0, rows(b, 1)]

    @pl.when(is_ocean)
    def _():
        top = fields[5, pl.ds(0, 1)]
        _, heat_now = light(own[0], top)
        heat[...] = heat_now

        def first_move(b):
            field_right(b).wait_recv()
            field_left(b).wait_recv()
            move_ocean(b, [fields[i, levels(b)] for i in range(4)], left_field, right_field)

        def first_stir(b):
            act = level_index(b) < wet
            weights = stir(b, fields[4, levels(b)])
            lag[0, rows(b)] = stirred(0, b, weights) + heat[levels(b)]
            for i in range(1, 4):
                lag[i, rows(b)] = jnp.where(act, stirred(i, b, weights), 0.0)
            for copy in second_halo(b, 4):
                copy.start()

        staged(first_move, first_stir)

        ready_wait(ready_partner)
        sun_copy().start()
        run(lag_copy, "start")

        @pl.when(first)
        def _():
            ready_wait(ready_cross)
            cross_wet()[1].start()
            run(lambda b: cross_tracer(b)[1], "start")

        def second_move(b):
            second_halo_wait(b, 4)
            warm = jnp.where(level_index(b) < wet, lag[0, rows(b)], 0.0)
            move_ocean(b, [warm] + [lag[i, rows(b)] for i in range(1, 4)], left_one, right_one)

        def second_stir(b):
            act = level_index(b) < wet
            weights = stir(b, jnp.where(act, lag_mixing(b), 0.0))
            shade[rows(b)] = stirred(0, b, weights)
            for i in range(1, 4):
                ocean_out[i, levels(b)] = jnp.where(act, stirred(i, b, weights), 0.0)

        staged(second_move, second_stir)

        @pl.when(early)
        def _():
            def chl_move(b):
                given_copy(b).wait_recv()
                first_halo_wait(b)
                move_tracers(
                    b, given[0, levels(b)], given[1, levels(b)],
                    left_in, lambda i: own[i, levels(b)], right_in,
                )

            def chl_stir(b):
                weights = stir(b, given[2, levels(b)])
                chl_got[levels(b)] = chl_after(b, weights, given[3, levels(b)])

            staged(chl_move, chl_stir)

        @pl.when(late)
        def _():
            run(chl_copy, "wait_recv")

        chl = chl_got[...]
        chl_out[...] = chl
        top_two = jnp.where(wet_in[...] > 0, fields[5, pl.ds(0, 1)], 0.0)
        shade_two, heat_two = light(chl, top_two)
        warm = shade[pl.ds(PAD, LEV)] + heat_two
        shade[pl.ds(PAD, LEV)] = warm
        below = shade[pl.ds(PAD + 1, LEV)]
        level = lax.broadcasted_iota(jnp.int32, (LEV, COL), 0)
        act = level < wet_in[...]
        ocean_out[0] = jnp.where(act, warm, 0.0)
        ocean_out[4] = jnp.where(jnp.logical_and(act, level < LEV - 1), warm - below, 0.0)
        ocean_out[5] = jnp.where(act, shade_two, 0.0)

    @pl.when(is_bgc)
    def _():
        def first_move(b):
            first_halo_wait(b)
            move_tracers(
                b, fields[2, levels(b)], fields[3, levels(b)],
                left_in, lambda i: own[i, levels(b)], right_in,
            )

        def first_stir(b):
            act = level_index(b) < wet
            weights = stir(b, fields[4, levels(b)])
            rate = fields[5, levels(b)]
            bent = []
            for i in range(NT):
                y = stirred(i, b, weights)
                one[b, i] = y
                bent.append(jnp.tanh(y))
            for i in range(NT):
                growth = reaction[i, 0] * bent[0]
                for j in range(1, NT):
                    growth = growth + reaction[i, j] * bent[j]
                one[b, i] = jnp.where(act, one[b, i] + rate * growth, 0.0)

            @when(first, b == 0)
            def _():
                ready_wait(ready_turn)

            for copy in second_halo(b, NT):
                copy.start()

            @pl.when(late)
            def _():
                chl_copy(b).start()

        staged(first_move, first_stir)

        sun_copy().wait_recv()
        shade_now, _ = light(own[0], sun[pl.ds(0, 1)])
        shade[pl.ds(PAD, LEV)] = shade_now

        def second_move(b):
            lag_copy(b).wait_recv()
            second_halo_wait(b, NT)
            move_tracers(
                b, lag[2, rows(b)], lag[3, rows(b)], left_one, lambda i: one[b, i], right_one
            )

        def second_stir(b):
            level = level_index(b)
            act = level < wet
            mixing = jnp.where(jnp.logical_and(act, level < LEV - 1), lag_mixing(b), 0.0)
            weights = stir(b, mixing)
            warm = jnp.where(act, lag[0, rows(b)], 0.0)
            sunlight = jnp.where(act, shade[rows(b)], 0.0)
            ocean_out[0, levels(b)] = warm
            for i in range(1, 4):
                ocean_out[i, levels(b)] = lag[i, rows(b)]
            ocean_out[4, levels(b)] = mixing
            ocean_out[5, levels(b)] = sunlight
            rate = 0.5 * sunlight * jax.nn.sigmoid(warm + 0.5 * lag[1, rows(b)])
            chl_out[levels(b)] = chl_after(b, weights, rate)

        staged(second_move, second_stir)

    @pl.when(is_ocean)
    def _():
        wet_right_copy().wait_send()
        wet_left_copy().wait_send()
        sun_copy().wait_send()

        @pl.when(is_early(right))
        def _():
            run(tracer_right, "wait_send")

        @pl.when(is_early(left))
        def _():
            run(tracer_left, "wait_send")

        @pl.when(jnp.logical_or(first, last))
        def _():
            cross_wet()[0].wait_send()
            run(lambda b: cross_tracer(b)[0], "wait_send")

        def drain(b):
            for copy in (field_right(b), field_left(b), lag_copy(b)) + second_halo(b, 4):
                copy.wait_send()

        each(drain)

    @pl.when(is_bgc)
    def _():
        @pl.when(not_last)
        def _():
            wet_right_copy().wait_send()
            run(tracer_right, "wait_send")

        @pl.when(not_first)
        def _():
            wet_left_copy().wait_send()
            run(tracer_left, "wait_send")

        @pl.when(early)
        def _():
            run(given_copy, "wait_send")

        @pl.when(late)
        def _():
            run(chl_copy, "wait_send")

        def drain(b):
            for copy in second_halo(b, NT):
                copy.wait_send()

        each(drain)


def per_device(ocean_fields, tracers, reaction, wet_levels, neighbours):
    f32, vmem = jnp.float32, pltpu.VMEM
    in_vmem = pl.BlockSpec(memory_space=vmem)
    in_hbm = pl.BlockSpec(memory_space=pltpu.HBM)
    dma, regular = pltpu.SemaphoreType.DMA, pltpu.SemaphoreType.REGULAR
    ocean_out, chl_out = pl.pallas_call(
        functools.partial(kernel, lax.axis_size("tile")),
        out_shape=(
            jax.ShapeDtypeStruct((6, LEV, COL), f32),
            jax.ShapeDtypeStruct((LEV, COL), f32),
        ),
        in_specs=[in_hbm] * 5,
        out_specs=(in_vmem, in_vmem),
        scratch_shapes=[
            vmem((6, LEV, COL), f32),
            vmem((NT, LEV, COL), f32),
            vmem((NB, 4, LB, COL), f32),
            vmem((NB, 4, LB, COL), f32),
            vmem((NB, NT, LB, COL), f32),
            vmem((NB, NT, LB, COL), f32),
            vmem((NB, NT, LB, COL), f32),
            vmem((NB, NT, LB, COL), f32),
            vmem((NB, NT, LB, COL), f32),
            vmem((NT, LEV + 2 * PAD, COL), f32),
            vmem((LEV + 2 * PAD, COL), f32),
            vmem((4, LEV + 2 * PAD, COL), f32),
            vmem((LB, COL), f32),
            vmem((LEV + 2 * PAD, COL), f32),
            vmem((LEV, COL), f32),
            vmem((4, LEV, COL), f32),
            vmem((LEV, COL), f32),
            vmem((1, COL), jnp.int32),
            vmem((3, COL), jnp.int32),
            vmem((1, COL), jnp.int32),
            vmem((1, COL), jnp.int32),
            pltpu.SMEM((NT, NT), f32),
            dma((5,)),
            dma((3, 2, NB)),
            dma((3, 2, NB)),
            dma((2,)),
            dma((2,)),
            dma((NB,)),
            dma((NB,)),
            dma((NB,)),
            dma((NB,)),
            dma,
            dma,
            dma((NB,)),
            dma,
            regular,
            regular,
            regular,
        ],
        compiler_params=pltpu.CompilerParams(
            collective_id=0, has_side_effects=True, vmem_limit_bytes=64 * 2**20
        ),
    )(ocean_fields[0], tracers, reaction, wet_levels[None, :], neighbours)
    return ocean_out[None], chl_out[None]


def solution(mesh):
    return jax.shard_map(
        per_device,
        mesh=mesh,
        in_specs=(
            P("comp", None, None, "tile"),
            P(None, None, "tile"),
            P(),
            P("tile"),
            P(None, "tile"),
        ),
        out_specs=(P("comp", None, None, "tile"), P("comp", None, "tile")),
        check_vma=False,
    )
```

time: 59.6 us -> 52.2 us (0.88)
  the two profiles are of different devices: /device:TPU:6 before, /device:TPU:512 now
where the time goes in v2:
time: 52.2 us; the launch traced here: 52.1 us
  Pallas kernels  49.2 us (94%)
  local copies, waits for them, and re-layouts  2.24 us (4%)
  between operations  0.65 us (1%)
    pallas_call x1, Pallas kernels, per_device(): pl.pallas_call(functools.partial(kernel, lax.axis_size('tile')), out_shap...  49.2 us
    unnamed x4, local copies, waits for them, and re-layouts  2.24 us

profile of v2, /device:TPU:512, one launch (start us, length us, event | category | flops | bytes accessed | tf_op | source)
XLA Modules:
  0.0 52.1 jit_solution(9800754983899687630)
XLA Ops:
  0.6 49.2 %shard_map.68 = (f32[6,64,128]{2,1,0:T(8,128)}, f32[64,128]{1,0:T(8,128)}) custom-call(f32[6,64,128]{2,1,0:T(8,128)} %bitcast.5, f32[19,64,128]{2,1,0:T(8,128)} %tracer_hbm.1, f32[19,19]{1,0:T(8,128)} %reaction_hbm.1, s32[1,128]{1,0:T(1,128)} %bitcast.7, s32[3,128]{1,0:T(4,128)} %near_hbm.1), custom_call_target="tpu_custom_call" | custom-call | tf_op jit(solution)/shard_map/pallas_call | solution.py:588
  49.8 0.0 copy-start
  49.8 1.6 %copy.9 = f32[1,6,64,128]{3,2,1,0:T(8,128)} copy(f32[1,6,64,128]{3,2,1,0:T(8,128)} %bitcast.4) | data formatting | bytes 393216
  51.4 0.0 copy-done
  51.4 0.6 %copy.10 = f32[1,64,128]{2,1,0:T(8,128)} copy(f32[1,64,128]{2,1,0:T(8,128)S(1)} %bitcast.6) | data formatting | bytes 65536
Async XLA Ops:
  49.8 1.6 %copy-start = (f32[64,128]{1,0:T(8,128)S(1)}, f32[64,128]{1,0:T(8,128)}, u32[]{:S(2)}) copy-start(f32[64,128]{1,0:T(8,128)} %get-tuple-element.5) | copy-start | bytes 98308

commit v3 on v2

--- a/solution.py
+++ b/solution.py
@@ -20,7 +20,7 @@
 TURN = 128
 SPAN = 16
 DEPTH = 8
-EARLY = 4
+EARLY = 8
 
 ROTATE_COS = math.cos(0.3)
 ROTATE_SIN = math.sin(0.3)
@@ -63,8 +63,8 @@
     n, ocean_hbm, tracer_hbm, reaction_hbm, wet_hbm, near_hbm, ocean_out, chl_out,
     fields, own, left_field, right_field, left_in, right_in, one, left_one, right_one,
     moved, link, lag, sun, shade, heat, given, chl_got, wet_in, near_in, wet_left, wet_right,
-    reaction, load_sem, halo_send, halo_recv, wet_send, wet_recv, comp_send, comp_recv,
-    given_send, given_recv, sun_send, sun_recv, cross_send, cross_wet_send,
+    far_field, far_chl, far_sun, far_near, far_wet, reaction, load_sem, halo_send, halo_recv, wet_send, wet_recv, comp_send, comp_recv,
+    given_send, given_recv, sun_send, sun_recv, cross_send, cross_wet_send, far_send, far_recv,
     ready_partner, ready_turn, ready_cross,
 ):
     turn = min(TURN, n)
@@ -76,13 +76,22 @@
     is_ocean = comp == 0
     is_bgc = jnp.logical_not(is_ocean)
     place = lax.rem(tile, turn)
-    first, last = place == 0, place == turn - 1
+    first, last, fore = place == 0, place == turn - 1, place == turn - 2
+    seam = jnp.logical_and(is_ocean, tile == 0)
+    before_seam = jnp.logical_and(is_ocean, tile == n - 1)
     not_first, not_last = jnp.logical_not(first), jnp.logical_not(last)
 
     def is_early(t):
-        return lax.rem(lax.div(t, SPAN), DEPTH) < EARLY
+        return jnp.logical_and(lax.rem(lax.div(t, SPAN), DEPTH) < EARLY, t != 1)
 
     early = is_early(tile)
+    column, odd = lax.rem(lax.div(tile, 2), max(SPAN // 2, 1)), lax.rem(lax.div(tile, SPAN), 2) == 1
+    first_column, last_column = column == 0, column == max(SPAN // 2, 1) - 1
+    held = jnp.logical_or(
+        jnp.logical_and(first_column, odd), jnp.logical_and(last_column, jnp.logical_not(odd))
+    )
+    held = jnp.logical_or(held, jnp.logical_and(last_column, tile >= n - turn))
+    held = jnp.logical_and(held, early)
     late = jnp.logical_not(early)
 
     def remote(src, dst, send, recv, device):
@@ -115,7 +124,7 @@
     barrier = pltpu.get_barrier_semaphore()
     signal(barrier, to_left)
 
-    @pl.when(not_last)
+    @pl.when(jnp.logical_or(not_last, before_seam))
     def _():
         signal(barrier, to_right)
 
@@ -130,11 +139,14 @@
         @pl.when(first)
         def _():
             signal(barrier, (1, left))
+            signal(barrier, (0, lax.rem(tile + n - 2, n)))
 
     turned = jnp.logical_or(first, last).astype(jnp.int32)
-    pl.semaphore_wait(barrier, 2 - first.astype(jnp.int32) + comp * (1 + turned))
-
-    @pl.when(last)
+    greeted = comp * (1 + turned) + (1 - comp) * fore.astype(jnp.int32)
+    late_turn = jnp.logical_and(first, jnp.logical_not(seam))
+    pl.semaphore_wait(barrier, 2 - late_turn.astype(jnp.int32) + greeted)
+
+    @when(last, jnp.logical_not(before_seam))
     def _():
         signal(ready_turn, to_right)
 
@@ -165,7 +177,7 @@
         return remote(tracer_hbm.at[:, levels(b)], right_in.at[b], send, halo_recv.at[0, 1, b], device)
 
     def field_right(b):
-        source = ocean_hbm.at[pl.ds(0, 4), levels(b)]
+        source = ocean_hbm.at[pl.ds(0, 5), levels(b)]
         return remote(source, left_field.at[b], halo_send.at[2, 0, b], halo_recv.at[2, 0, b], to_right)
 
     def field_left(b):
@@ -194,15 +206,29 @@
     def sun_copy():
         return remote(ocean_hbm.at[5, pl.ds(0, LB)], sun, sun_send, sun_recv, partner)
 
+    def far_copies():
+        pairs = (
+            (near_in, far_near),
+            (ocean_hbm.at[5, pl.ds(0, LB)], far_sun),
+            (tracer_hbm.at[0], far_chl),
+        )
+        return [remote(a, b, far_send.at[i], far_recv.at[i], to_right) for i, (a, b) in enumerate(pairs)]
+
+    def fore_copies():
+        after_next = (comp, lax.rem(tile + 2, n))
+        pairs = ((wet_in, far_wet), (ocean_hbm.at[pl.ds(0, 4)], far_field))
+        return [remote(a, b, far_send.at[i], far_recv.at[3 + i], after_next) for i, (a, b) in enumerate(pairs)]
+
     def cross_wet():
         if_last = remote(wet_in, wet_left, cross_wet_send, wet_recv.at[0], (1, right))
         if_first = remote(wet_in, wet_right, cross_wet_send, wet_recv.at[1], (1, left))
         return if_last, if_first
 
     def cross_tracer(b):
+        other = 1 - comp
         return (
-            tracer_right(b, (1, right), cross_send.at[b]),
-            tracer_left(b, (1, left), cross_send.at[b]),
+            tracer_right(b, (other, right), cross_send.at[b]),
+            tracer_left(b, (other, left), cross_send.at[b]),
         )
 
     def each(body):
@@ -215,24 +241,36 @@
         pl.semaphore_wait(semaphore, 1)
 
     loads[0].wait()
+    loads[1].wait()
 
     @pl.when(is_ocean)
     def _():
         wet_right_copy().start()
+
+        @pl.when(last)
+        def _():
+            for copy in far_copies():
+                copy.start()
+
         run(field_right, "start")
 
-        @pl.when(first)
+        @pl.when(fore)
+        def _():
+            for copy in fore_copies():
+                copy.start()
+
+        @pl.when(late_turn)
         def _():
             ready_wait(ready_turn)
 
         wet_left_copy().start()
         run(field_left, "start")
 
-        @pl.when(is_early(right))
+        @when(is_early(right), not_last)
         def _():
             run(tracer_right, "start")
 
-        @pl.when(is_early(left))
+        @when(is_early(left), not_first)
         def _():
             run(tracer_left, "start")
 
@@ -256,12 +294,26 @@
                 tracer_left(b).start()
 
         each(start_both)
+
+        @when(is_early(right), last)
+        def _():
+            run(lambda b: cross_tracer(b)[0], "start")
+
+        @when(is_early(left), first)
+        def _():
+            run(lambda b: cross_tracer(b)[1], "start")
 
     @when(is_ocean, last)
     def _():
         ready_wait(ready_cross)
         cross_wet()[0].start()
         run(lambda b: cross_tracer(b)[0], "start")
+
+    @when(is_ocean, first)
+    def _():
+        ready_wait(ready_cross)
+        cross_wet()[1].start()
+        run(lambda b: cross_tracer(b)[1], "start")
 
     zero = jnp.zeros((PAD, COL), jnp.float32)
     link[pl.ds(0, PAD)] = zero
@@ -272,7 +324,7 @@
         moved[i, pl.ds(0, PAD)] = zero
         moved[i, pl.ds(PAD + LEV, PAD)] = zero
 
-    for copy in loads[1:]:
+    for copy in loads[2:]:
         copy.wait()
 
     def growth_rate(b):
@@ -290,39 +342,46 @@
 
         each(rate)
 
-    wet = jnp.broadcast_to(wet_in[...], (LB, COL))
-    near = [jnp.broadcast_to(near_in[pl.ds(k, 1), :], (LB, COL)) for k in range(3)]
-    index = [jnp.bitwise_and(p, COL - 1) for p in near]
-    in_left = [p < COL for p in near]
-    in_right = [p >= 2 * COL for p in near]
-
-    def reach(k, at_left, at_own, at_right):
-        inner = jnp.where(in_right[k], lane_take(at_right, index[k]), lane_take(at_own, index[k]))
-        return jnp.where(in_left[k], lane_take(at_left, index[k]), inner)
+    def geography(wet_own, near_rows, wet_at_left, wet_at_right):
+        near = [jnp.broadcast_to(near_rows[pl.ds(k, 1), :], (LB, COL)) for k in range(3)]
+        index = [jnp.bitwise_and(p, COL - 1) for p in near]
+        in_left = [p < COL for p in near]
+        in_right = [p >= 2 * COL for p in near]
+
+        def reach(k, at_left, at_own, at_right):
+            inner = jnp.where(
+                in_right[k], lane_take(at_right, index[k]), lane_take(at_own, index[k])
+            )
+            return jnp.where(in_left[k], lane_take(at_left, index[k]), inner)
+
+        wet, wet_l, wet_r = (
+            jnp.broadcast_to(w[...], (LB, COL)) for w in (wet_own, wet_at_left, wet_at_right)
+        )
+        wet_near = [jnp.minimum(reach(k, wet_l, wet, wet_r), wet) for k in range(3)]
+        return wet, wet_near, reach
 
     wet_right_copy().wait_recv()
     wet_left_copy().wait_recv()
-    wet_l = jnp.broadcast_to(wet_left[...], (LB, COL))
-    wet_r = jnp.broadcast_to(wet_right[...], (LB, COL))
-    wet_near = [jnp.minimum(reach(k, wet_l, wet, wet_r), wet) for k in range(3)]
-
-    def face_weights(b, east, north):
+    here = geography(wet_in, near_in, wet_left, wet_right)
+    wet = here[0]
+
+    def face_weights(b, east, north, land=here):
         level = level_index(b)
         found = []
         for k in range(3):
             angle = 2.0 * math.pi * k / 3.0
             w = 0.05 + 0.25 * jax.nn.sigmoid(east * math.cos(angle) + north * math.sin(angle))
-            found.append(jnp.where(level < wet_near[k], w, 0.0))
+            found.append(jnp.where(level < land[1][k], w, 0.0))
         return found
 
-    def move(weights, stay, at_left, at_own, at_right):
+    def move(weights, stay, at_left, at_own, at_right, land=here):
         total = stay * at_own
         for k in range(3):
-            total = total + weights[k] * reach(k, at_left, at_own, at_right)
+            total = total + weights[k] * land[2](k, at_left, at_own, at_right)
         return total
 
-    def stir(b, mixing):
-        below = jnp.where(level_index(b) + 1 < wet, 0.02 + 0.13 * jax.nn.sigmoid(mixing), 0.0)
+    def stir(b, mixing, land=here):
+        below = jnp.where(level_index(b) + 1 < land[0], 0.02 + 0.13 * jax.nn.sigmoid(mixing), 0.0)
         link[rows(b)] = below
         above = link[rows(b, -1)]
         return 1.0 - below - above, below, above
@@ -348,13 +407,14 @@
 
         lax.fori_loop(0, NB + 1, body, 0)
 
-    def move_ocean(b, state, at_left, at_right):
-        weights = face_weights(b, state[2], state[3])
-        steady = [jnp.where(level_index(b) < wet_near[k], 0.15, 0.0) for k in range(3)]
+    def move_ocean(b, state, at_left, at_right, land=here):
+        weights = face_weights(b, state[2], state[3], land)
+        steady = [jnp.where(level_index(b) < land[1][k], 0.15, 0.0) for k in range(3)]
         q = []
         for i in range(4):
             w = weights if i < 2 else steady
-            q.append(move(w, 1.0 - w[0] - w[1] - w[2], at_left[b, i], state[i], at_right[b, i]))
+            stay = 1.0 - w[0] - w[1] - w[2]
+            q.append(move(w, stay, at_left(i), state[i], at_right(i), land))
         moved[0, rows(b)] = q[0]
         moved[1, rows(b)] = q[1]
         moved[2, rows(b)] = ROTATE_COS * q[2] + ROTATE_SIN * q[3]
@@ -370,8 +430,8 @@
         tracer_right(b).wait_recv()
         tracer_left(b).wait_recv()
 
-    def second_halo_wait(b, count):
-        for copy in second_halo(b, count):
+    def second_halo_wait(b):
+        for copy in second_halo(b, NT):
             copy.wait_recv()
 
     def chl_after(b, weights, rate):
@@ -393,7 +453,10 @@
         def first_move(b):
             field_right(b).wait_recv()
             field_left(b).wait_recv()
-            move_ocean(b, [fields[i, levels(b)] for i in range(4)], left_field, right_field)
+            move_ocean(
+                b, [fields[i, levels(b)] for i in range(4)],
+                lambda i: left_field[b, i], lambda i: right_field[b, i],
+            )
 
         def first_stir(b):
             act = level_index(b) < wet
@@ -401,25 +464,57 @@
             lag[0, rows(b)] = stirred(0, b, weights) + heat[levels(b)]
             for i in range(1, 4):
                 lag[i, rows(b)] = jnp.where(act, stirred(i, b, weights), 0.0)
-            for copy in second_halo(b, 4):
-                copy.start()
+            to_the_right, to_the_left = second_halo(b, 4)
+            to_the_left.start()
+
+            @pl.when(not_last)
+            def _():
+                to_the_right.start()
 
         staged(first_move, first_stir)
 
         ready_wait(ready_partner)
         sun_copy().start()
-        run(lag_copy, "start")
+
+        @pl.when(jnp.logical_not(held))
+        def _():
+            run(lag_copy, "start")
 
         @pl.when(first)
         def _():
-            ready_wait(ready_cross)
-            cross_wet()[1].start()
-            run(lambda b: cross_tracer(b)[1], "start")
+            for copy in far_copies() + fore_copies():
+                copy.wait_recv()
+            far = geography(wet_left, far_near, far_wet, wet_in)
+            heat[...] = light(far_chl[...], far_sun[pl.ds(0, 1)])[1]
+
+            def far_move(b):
+                move_ocean(
+                    b, [left_field[b, i] for i in range(4)],
+                    lambda i: far_field[i, levels(b)], lambda i: fields[i, levels(b)], far,
+                )
+
+            def far_stir(b):
+                act = level_index(b) < far[0]
+                weights = stir(b, left_field[b, 4], far)
+                left_one[b, 0] = stirred(0, b, weights) + heat[levels(b)]
+                for i in range(1, 4):
+                    left_one[b, i] = jnp.where(act, stirred(i, b, weights), 0.0)
+
+            staged(far_move, far_stir)
+
 
         def second_move(b):
-            second_halo_wait(b, 4)
+            second_halo(b, 4)[1].wait_recv()
+
+            @pl.when(not_first)
+            def _():
+                second_halo(b, 4)[0].wait_recv()
+
             warm = jnp.where(level_index(b) < wet, lag[0, rows(b)], 0.0)
-            move_ocean(b, [warm] + [lag[i, rows(b)] for i in range(1, 4)], left_one, right_one)
+            move_ocean(
+                b, [warm] + [lag[i, rows(b)] for i in range(1, 4)],
+                lambda i: left_one[b, i], lambda i: right_one[b, i],
+            )
 
         def second_stir(b):
             act = level_index(b) < wet
@@ -434,6 +529,11 @@
         def _():
             def chl_move(b):
                 given_copy(b).wait_recv()
+
+                @when(held, b == 0)
+                def _():
+                    run(lag_copy, "start")
+
                 first_halo_wait(b)
                 move_tracers(
                     b, given[0, levels(b)], given[1, levels(b)],
@@ -487,18 +587,23 @@
                     growth = growth + reaction[i, j] * bent[j]
                 one[b, i] = jnp.where(act, one[b, i] + rate * growth, 0.0)
 
-            @when(first, b == 0)
-            def _():
-                ready_wait(ready_turn)
-
-            for copy in second_halo(b, NT):
-                copy.start()
+            to_the_right, to_the_left = second_halo(b, NT)
+            to_the_right.start()
+
+            @pl.when(not_first)
+            def _():
+                to_the_left.start()
 
             @pl.when(late)
             def _():
                 chl_copy(b).start()
 
         staged(first_move, first_stir)
+
+        @pl.when(first)
+        def _():
+            ready_wait(ready_turn)
+            run(lambda b: second_halo(b, NT)[1], "start")
 
         sun_copy().wait_recv()
         shade_now, _ = light(own[0], sun[pl.ds(0, 1)])
@@ -506,7 +611,7 @@
 
         def second_move(b):
             lag_copy(b).wait_recv()
-            second_halo_wait(b, NT)
+            second_halo_wait(b)
             move_tracers(
                 b, lag[2, rows(b)], lag[3, rows(b)], left_one, lambda i: one[b, i], right_one
             )
@@ -534,11 +639,11 @@
         wet_left_copy().wait_send()
         sun_copy().wait_send()
 
-        @pl.when(is_early(right))
+        @when(is_early(right), not_last)
         def _():
             run(tracer_right, "wait_send")
 
-        @pl.when(is_early(left))
+        @when(is_early(left), not_first)
         def _():
             run(tracer_left, "wait_send")
 
@@ -548,10 +653,24 @@
             run(lambda b: cross_tracer(b)[0], "wait_send")
 
         def drain(b):
-            for copy in (field_right(b), field_left(b), lag_copy(b)) + second_halo(b, 4):
+            for copy in (field_right(b), field_left(b), lag_copy(b), second_halo(b, 4)[1]):
                 copy.wait_send()
 
+            @pl.when(not_last)
+            def _():
+                second_halo(b, 4)[0].wait_send()
+
         each(drain)
+
+        @pl.when(last)
+        def _():
+            for copy in far_copies():
+                copy.wait_send()
+
+        @pl.when(fore)
+        def _():
+            for copy in fore_copies():
+                copy.wait_send()
 
     @pl.when(is_bgc)
     def _():
@@ -564,6 +683,14 @@
         def _():
             wet_left_copy().wait_send()
             run(tracer_left, "wait_send")
+
+        @when(is_early(right), last)
+        def _():
+            run(lambda b: cross_tracer(b)[0], "wait_send")
+
+        @when(is_early(left), first)
+        def _():
+            run(lambda b: cross_tracer(b)[1], "wait_send")
 
         @pl.when(early)
         def _():
@@ -596,7 +723,7 @@
         scratch_shapes=[
             vmem((6, LEV, COL), f32),
             vmem((NT, LEV, COL), f32),
-            vmem((NB, 4, LB, COL), f32),
+            vmem((NB, 5, LB, COL), f32),
             vmem((NB, 4, LB, COL), f32),
             vmem((NB, NT, LB, COL), f32),
             vmem((NB, NT, LB, COL), f32),
@@ -615,6 +742,11 @@
             vmem((3, COL), jnp.int32),
             vmem((1, COL), jnp.int32),
             vmem((1, COL), jnp.int32),
+            vmem((4, LEV, COL), f32),
+            vmem((LEV, COL), f32),
+            vmem((LB, COL), f32),
+            vmem((3, COL), jnp.int32),
+            vmem((1, COL), jnp.int32),
             pltpu.SMEM((NT, NT), f32),
             dma((5,)),
             dma((3, 2, NB)),
@@ -629,6 +761,8 @@
             dma,
             dma((NB,)),
             dma,
+            dma((3,)),
+            dma((5,)),
             regular,
             regular,
             regular,

time: 52.2 us -> 47 us (0.900)
  the two profiles are of different devices: /device:TPU:512 before, /device:TPU:6 now
where the time goes in v3:
time: 47 us; the launch traced here: 46.8 us
  Pallas kernels  43.9 us (93%)
  local copies, waits for them, and re-layouts  2.24 us (5%)
  between operations  0.65 us (1%)
    pallas_call x1, Pallas kernels, per_device(): pl.pallas_call(functools.partial(kernel, lax.axis_size('tile')), out_shap...  43.9 us
    unnamed x4, local copies, waits for them, and re-layouts  2.24 us

profile of v3, /device:TPU:6, one launch (start us, length us, event | category | flops | bytes accessed | tf_op | source)
XLA Modules:
  0.0 46.8 jit_solution(5116193190367719159)
XLA Ops:
  0.6 43.9 %shard_map.68 = (f32[6,64,128]{2,1,0:T(8,128)}, f32[64,128]{1,0:T(8,128)}) custom-call(f32[6,64,128]{2,1,0:T(8,128)} %bitcast.5, f32[19,64,128]{2,1,0:T(8,128)} %tracer_hbm.1, f32[19,19]{1,0:T(8,128)} %reaction_hbm.1, s32[1,128]{1,0:T(1,128)} %bitcast.7, s32[3,128]{1,0:T(4,128)} %near_hbm.1), custom_call_target="tpu_custom_call" | custom-call | tf_op jit(solution)/shard_map/pallas_call | solution.py:715
  44.6 0.0 copy-start
  44.6 1.6 %copy.9 = f32[1,6,64,128]{3,2,1,0:T(8,128)} copy(f32[1,6,64,128]{3,2,1,0:T(8,128)} %bitcast.4) | data formatting | bytes 393216
  46.2 0.0 copy-done
  46.2 0.6 %copy.10 = f32[1,64,128]{2,1,0:T(8,128)} copy(f32[1,64,128]{2,1,0:T(8,128)S(1)} %bitcast.6) | data formatting | bytes 65536
Async XLA Ops:
  44.6 1.6 %copy-start = (f32[64,128]{1,0:T(8,128)S(1)}, f32[64,128]{1,0:T(8,128)}, u32[]{:S(2)}) copy-start(f32[64,128]{1,0:T(8,128)} %get-tuple-element.5) | copy-start | bytes 98308

commit v4 on v3

--- a/solution.py
+++ b/solution.py
@@ -82,7 +82,7 @@
     not_first, not_last = jnp.logical_not(first), jnp.logical_not(last)
 
     def is_early(t):
-        return jnp.logical_and(lax.rem(lax.div(t, SPAN), DEPTH) < EARLY, t != 1)
+        return jnp.logical_and(lax.rem(lax.div(t, SPAN), DEPTH) < EARLY, (t != 1) & (lax.rem(t, turn) != 0))
 
     early = is_early(tile)
     column, odd = lax.rem(lax.div(tile, 2), max(SPAN // 2, 1)), lax.rem(lax.div(tile, SPAN), 2) == 1
@@ -768,7 +768,7 @@
             regular,
         ],
         compiler_params=pltpu.CompilerParams(
-            collective_id=0, has_side_effects=True, vmem_limit_bytes=64 * 2**20
+            collective_id=0, has_side_effects=True, vmem_limit_bytes=56229888
         ),
     )(ocean_fields[0], tracers, reaction, wet_levels[None, :], neighbours)
     return ocean_out[None], chl_out[None]

time: 47 us -> 46.5 us (0.989)
  the two profiles are of different devices: /device:TPU:6 before, /device:TPU:1 now
where the time goes in v4:
time: 46.5 us; the launch traced here: 46.3 us
  Pallas kernels  42.9 us (92%)
  local copies, waits for them, and re-layouts  2.67 us (6%)
  between operations  0.66 us (1%)
    pallas_call x1, Pallas kernels, per_device(): pl.pallas_call(functools.partial(kernel, lax.axis_size('tile')), out_shap...  42.9 us
    unnamed x8, local copies, waits for them, and re-layouts  2.67 us

profile of v4, /device:TPU:1, one launch (start us, length us, event | category | flops | bytes accessed | tf_op | source)
XLA Modules:
  0.0 46.3 jit_solution(8245575207540162742)
XLA Ops:
  0.6 0.0 copy-start.1
  0.6 0.0 copy-start.2
  0.7 0.7 %copy-done.1 = s32[3,128]{1,0:T(4,128)S(1)} copy-done((s32[3,128]{1,0:T(4,128)S(1)}, s32[3,128]{1,0:T(4,128)}, u32[]{:S(2)}) %copy-start.1) | copy-done | bytes 1560
  1.3 0.0 copy-done.2
  1.3 0.0 copy-start
  1.3 0.7 %copy-done = f32[19,19]{1,0:T(8,128)S(1)} copy-done((f32[19,19]{1,0:T(8,128)S(1)}, f32[19,19]{1,0:T(8,128)}, u32[]{:S(2)}) %copy-start) | copy-done | bytes 1468
  2.0 42.9 %shard_map.68 = (f32[6,64,128]{2,1,0:T(8,128)S(1)}, f32[64,128]{1,0:T(8,128)S(1)}) custom-call(f32[6,64,128]{2,1,0:T(8,128)} %bitcast.7, f32[19,64,128]{2,1,0:T(8,128)} %tracer_hbm.1, f32[19,19]{1,0:T(8,128)S(1)} %copy-done, s32[1,128]{1,0:T(1,128)S(1)} %bitcast.6, s32[3,128]{1,0:T(4,128)S(1)} %copy-done.1), custom_call_target="tpu_custom_call" | custom-call | tf_op jit(solution)/shard_map/pallas_call | solution.py:715
  45.0 0.7 %copy.9 = f32[1,6,64,128]{3,2,1,0:T(8,128)} copy(f32[1,6,64,128]{3,2,1,0:T(8,128)S(1)} %bitcast.4) | data formatting | bytes 393216
  45.7 0.6 %copy.10 = f32[1,64,128]{2,1,0:T(8,128)} copy(f32[1,64,128]{2,1,0:T(8,128)S(1)} %bitcast.5) | data formatting | bytes 65536
Async XLA Ops:
  0.6 0.7 %copy-start.1 = (s32[3,128]{1,0:T(4,128)S(1)}, s32[3,128]{1,0:T(4,128)}, u32[]{:S(2)}) copy-start(s32[3,128]{1,0:T(4,128)} %near_hbm.1) | copy-start | bytes 4612
  0.6 0.7 %copy-start.2 = (s32[128]{0:T(128)S(1)}, s32[128]{0:T(128)}, u32[]{:S(2)}) copy-start(s32[128]{0:T(128)} %param.8) | copy-start | bytes 1540
  1.3 0.7 %copy-start = (f32[19,19]{1,0:T(8,128)S(1)}, f32[19,19]{1,0:T(8,128)}, u32[]{:S(2)}) copy-start(f32[19,19]{1,0:T(8,128)} %reaction_hbm.1) | copy-start | bytes 4336

commit v5 on v4

--- a/solution.py
+++ b/solution.py
@@ -247,24 +247,24 @@
     def _():
         wet_right_copy().start()
 
+        run(field_right, "start")
+
+        @pl.when(fore)
+        def _():
+            for copy in fore_copies():
+                copy.start()
+
+        @pl.when(late_turn)
+        def _():
+            ready_wait(ready_turn)
+
+        wet_left_copy().start()
+        run(field_left, "start")
+
         @pl.when(last)
         def _():
             for copy in far_copies():
                 copy.start()
-
-        run(field_right, "start")
-
-        @pl.when(fore)
-        def _():
-            for copy in fore_copies():
-                copy.start()
-
-        @pl.when(late_turn)
-        def _():
-            ready_wait(ready_turn)
-
-        wet_left_copy().start()
-        run(field_left, "start")
 
         @when(is_early(right), not_last)
         def _():

time: 46.5 us -> 46.1 us (level)
  no operation moved by 1% of the time
where the time goes in v5:
time: 46.1 us; the launch traced here: 45.9 us
  Pallas kernels  42.5 us (92%)
  local copies, waits for them, and re-layouts  2.67 us (6%)
  between operations  0.66 us (1%)
    pallas_call x1, Pallas kernels, per_device(): pl.pallas_call(functools.partial(kernel, lax.axis_size('tile')), out_shap...  42.5 us
    unnamed x8, local copies, waits for them, and re-layouts  2.67 us

profile of v5, /device:TPU:1, one launch (start us, length us, event | category | flops | bytes accessed | tf_op | source)
XLA Modules:
  0.0 45.9 jit_solution(11446871831214946237)
XLA Ops:
  0.6 0.0 copy-start.1
  0.6 0.0 copy-start.2
  0.7 0.7 %copy-done.1 = s32[3,128]{1,0:T(4,128)S(1)} copy-done((s32[3,128]{1,0:T(4,128)S(1)}, s32[3,128]{1,0:T(4,128)}, u32[]{:S(2)}) %copy-start.1) | copy-done | bytes 1560
  1.3 0.0 copy-done.2
  1.3 0.0 copy-start
  1.3 0.7 %copy-done = f32[19,19]{1,0:T(8,128)S(1)} copy-done((f32[19,19]{1,0:T(8,128)S(1)}, f32[19,19]{1,0:T(8,128)}, u32[]{:S(2)}) %copy-start) | copy-done | bytes 1468
  2.0 42.5 %shard_map.68 = (f32[6,64,128]{2,1,0:T(8,128)S(1)}, f32[64,128]{1,0:T(8,128)S(1)}) custom-call(f32[6,64,128]{2,1,0:T(8,128)} %bitcast.7, f32[19,64,128]{2,1,0:T(8,128)} %tracer_hbm.1, f32[19,19]{1,0:T(8,128)S(1)} %copy-done, s32[1,128]{1,0:T(1,128)S(1)} %bitcast.6, s32[3,128]{1,0:T(4,128)S(1)} %copy-done.1), custom_call_target="tpu_custom_call" | custom-call | tf_op jit(solution)/shard_map/pallas_call | solution.py:715
  44.6 0.7 %copy.9 = f32[1,6,64,128]{3,2,1,0:T(8,128)} copy(f32[1,6,64,128]{3,2,1,0:T(8,128)S(1)} %bitcast.4) | data formatting | bytes 393216
  45.2 0.6 %copy.10 = f32[1,64,128]{2,1,0:T(8,128)} copy(f32[1,64,128]{2,1,0:T(8,128)S(1)} %bitcast.5) | data formatting | bytes 65536
Async XLA Ops:
  0.6 0.7 %copy-start.1 = (s32[3,128]{1,0:T(4,128)S(1)}, s32[3,128]{1,0:T(4,128)}, u32[]{:S(2)}) copy-start(s32[3,128]{1,0:T(4,128)} %near_hbm.1) | copy-start | bytes 4612
  0.6 0.7 %copy-start.2 = (s32[128]{0:T(128)S(1)}, s32[128]{0:T(128)}, u32[]{:S(2)}) copy-start(s32[128]{0:T(128)} %param.8) | copy-start | bytes 1540
  1.3 0.7 %copy-start = (f32[19,19]{1,0:T(8,128)S(1)}, f32[19,19]{1,0:T(8,128)}, u32[]{:S(2)}) copy-start(f32[19,19]{1,0:T(8,128)} %reaction_hbm.1) | copy-start | bytes 4336
